TPU v7x, 128 devices: a whole 4x4x4 slice. The times are simulated.
128 devices in a mesh: section: 2 (over x_lo), dp: 8 (over x_hi, y), tensor: 8 (over z, core).
Axes of the slice: x: 4 (x_hi: 2, x_lo: 2; x = x_hi * 2 + x_lo), y: 4, z: 4, core: 2. Of those that a mesh axis runs over, the one named last changes fastest.
Arguments:
- tokens: bfloat16 [2048, 8192], P('dp', ('section', 'tensor')), may hold values from -6 to 6
- segment_ids: int32 [8, 256], P('dp'), may hold values from 0 to 3, never falling along the last dimension, each value on 1 to 128 neighbouring positions
- gain_attn: float32 [8192], replicated, may hold values from 0.1 to 1.9
- w_query: bfloat16 [8192, 4096], P(None, ('section', 'tensor')), may hold values from -0.06629126 to 0.06629126
- w_key: bfloat16 [8192, 4096], P(None, ('section', 'tensor')), may hold values from -0.06629126 to 0.06629126
- w_value: bfloat16 [8192, 4096], P(None, ('section', 'tensor')), may hold values from -0.0625 to 0.0625
- w_output: bfloat16 [4096, 8192], P(('section', 'tensor')), may hold values from -0.09375 to 0.09375
- gain_ffn: float32 [8192], replicated, may hold values from 0.1 to 1.9
- w_up: bfloat16 [8192, 16384], P(('section', 'tensor'), 'dp'), may hold values from -0.0625 to 0.0625
- w_down: bfloat16 [16384, 8192], P('dp', ('section', 'tensor')), may hold values from -0.046875 to 0.046875
Outputs:
- layer_out: bfloat16 [2048, 8192], P('dp', ('section', 'tensor'))
Inputs may be any that keep to these rules, and one draw needn't show every extreme that they name: `segment_ids`: segment numbers never fall along a replica's tokens; each segment holds 1 to 128 tokens.
All inputs are finite; a program needn't handle non-finite values.
Results may differ from a plain program's by a relative error of at most 0.023.
Values may be sent and summed in bfloat16 or wider, within the bound.
A program may use at most 128 MiB of HBM per device.

v0:
```python
import jax
import jax.numpy as jnp
from jax import lax
from jax.sharding import PartitionSpec as P

HD = 128


def layer_norm(values, gain):
    mean = jnp.mean(values, axis=-1, keepdims=True)
    second = jnp.mean(values * values, axis=-1, keepdims=True)
    return (values - mean) * lax.rsqrt(second - mean * mean + 1e-05) * gain


def per_device(
    tokens, segment_ids, gain_attn, w_query, w_key, w_value, w_output, gain_ffn, w_up, w_down
):
    tok_rows = tokens.shape[0]
    width = gain_attn.shape[0]
    groups = lax.axis_size(("section", "tensor"))
    share = width // groups
    first_col = lax.axis_index(("section", "tensor")) * share
    whole = lax.all_gather(tokens, ("section", "tensor"), axis=1, tiled=True)
    normed = layer_norm(whole.astype(jnp.float32), gain_attn).astype(jnp.bfloat16)
    local_heads = w_query.shape[1] // HD
    query = jnp.dot(normed, w_query, preferred_element_type=jnp.float32).astype(jnp.bfloat16)
    key = jnp.dot(normed, w_key, preferred_element_type=jnp.float32).astype(jnp.bfloat16)
    value = jnp.dot(normed, w_value, preferred_element_type=jnp.float32).astype(jnp.bfloat16)
    query = query.reshape(tok_rows, local_heads, HD)
    key = key.reshape(tok_rows, local_heads, HD)
    value = value.reshape(tok_rows, local_heads, HD)
    scores = jnp.einsum("qhd,khd->hqk", query, key, preferred_element_type=jnp.float32) * HD ** (
        -0.5
    )
    position = jnp.arange(tok_rows)
    segment_row = segment_ids[0]
    keep = jnp.logical_and(
        position[:, None] >= position[None, :], segment_row[:, None] == segment_row[None, :]
    )
    scores = jnp.where(keep[None], scores, -1e30)
    top = jnp.max(scores, axis=-1, keepdims=True)
    expo = jnp.exp(scores - top)
    probs = (expo / jnp.sum(expo, axis=-1, keepdims=True)).astype(jnp.bfloat16)
    context = jnp.einsum("hqk,khd->qhd", probs, value, preferred_element_type=jnp.float32)
    context = context.astype(jnp.bfloat16).reshape(tok_rows, local_heads * HD)
    partial_out = jnp.dot(context, w_output, preferred_element_type=jnp.float32)
    summed = lax.psum(partial_out.astype(jnp.bfloat16), ("section", "tensor")).astype(jnp.float32)
    resid_full = (whole.astype(jnp.float32) + summed).astype(jnp.bfloat16)
    normed_full = layer_norm(resid_full.astype(jnp.float32), gain_ffn).astype(jnp.bfloat16)
    normed_ffn = lax.dynamic_slice_in_dim(normed_full, first_col, share, 1)
    resid_mid = lax.dynamic_slice_in_dim(resid_full, first_col, share, 1)
    gathered = lax.all_gather(normed_ffn, "dp", axis=0, tiled=True)
    pre_act = lax.psum_scatter(
        jnp.dot(gathered, w_up, preferred_element_type=jnp.float32).astype(jnp.bfloat16),
        ("section", "tensor"),
        scatter_dimension=0,
        tiled=True,
    ).astype(jnp.float32)
    activated = jax.nn.gelu(pre_act, approximate=True).astype(jnp.bfloat16)
    partial_down = jnp.dot(
        lax.all_gather(activated, ("section", "tensor"), axis=0, tiled=True),
        w_down,
        preferred_element_type=jnp.float32,
    )
    ffn_out = lax.psum_scatter(
        partial_down.astype(jnp.bfloat16), "dp", scatter_dimension=0, tiled=True
    ).astype(jnp.float32)
    return (resid_mid.astype(jnp.float32) + ffn_out).astype(jnp.bfloat16)


def solution(mesh):
    return jax.shard_map(
        per_device,
        mesh=mesh,
        in_specs=(
            P("dp", ("section", "tensor")),
            P("dp", None),
            P(),
            P(None, ("section", "tensor")),
            P(None, ("section", "tensor")),
            P(None, ("section", "tensor")),
            P(("section", "tensor"), None),
            P(),
            P(("section", "tensor"), "dp"),
            P("dp", ("section", "tensor")),
        ),
        out_specs=P("dp", ("section", "tensor")),
        check_vma=False,
    )
```

profile of v0, /device:TPU:0, one launch (start us, length us, event | category | flops | bytes accessed | tf_op | source)
XLA Modules:
  0.0 492.6 jit_solution(8370720796275052697)
XLA Ops:
  6.5 0.0 copy-start
  6.5 0.0 copy-start.7
  6.5 0.0 all-gather.4.cloned.1.call-start
  6.5 0.7 all-gather.4.cloned.1.call-update
  7.3 0.0 all-reduce.2.cloned.1.call-start
  7.3 0.9 fusion.18
  8.2 40.8 %all-gather.4.cloned.1.call-done = bf16[256,8192]{1,0:T(8,128)(2,1)} async-done(((bf16[256,512]{1,0:T(8,128)(2,1)}), bf16[256,8192]{1,0:T(8,128)(2,1)}) %all-gather.4.cloned.1.call-update) | async-done | bytes 4194320 | tf_op jit(solution)/shard_map/all_gather | solution.py:23
  49.0 0.0 copy-start.3
  49.0 3.5 convert_reduce_fusion
  52.5 0.0 copy-done.7
  52.5 0.0 copy-done.3
  52.5 0.0 copy-start.5
  52.5 1.8 fusion.3
  54.3 0.4 copy-done.5
  54.7 0.0 copy-start.2
  54.7 0.0 copy-start.6
  54.7 1.8 convolution_convert_fusion.4
  56.6 0.3 copy-done.2
  56.9 1.6 copy-done.6
  58.4 1.8 convolution_convert_fusion.5
  60.3 0.4 fusion.23
  60.7 0.3 fusion.8
  60.9 5.2 %convolution_convert_fusion.6 = bf16[256,256]{0,1:T(8,128)(2,1)S(1)} fusion(bf16[256,8192]{1,0:T(8,128)(2,1)} %copy-done.2, bf16[8192,256]{1,0:T(8,128)(2,1)} %param.15), kind=kOutput, calls=%fused_computation.26 | convolution fusion | flops 1073807360 | bytes 8519680 | tf_op jit(solution)/shard_map/dot_general | solution.py:28
  66.1 0.3 convolution_convert_fusion.3
  66.4 5.4 %convolution_convert_fusion = bf16[256,8192]{1,0:T(8,128)(2,1)} fusion(bf16[256,256]{0,1:T(8,128)(2,1)S(1)} %bitcast.30, bf16[256,8192]{1,0:T(8,128)(2,1)} %param.16), kind=kOutput, calls=%fused_computation.5 | convolution fusion | flops 1075838976 | bytes 8519680 | tf_op jit(solution)/shard_map/dot_general | solution.py:46
  71.9 0.0 all-reduce.2.cloned.1.call-update
  71.9 0.2 all-gather.6.cloned.1.call-start
  72.1 0.8 dynamic-slice
  72.9 128.7 %all-reduce.2.cloned.1.call-done = bf16[256,8192]{1,0:T(8,128)(2,1)} async-done(((bf16[256,8192]{1,0:T(8,128)(2,1)}), bf16[256,8192]{1,0:T(8,128)(2,1)}) %all-reduce.2.cloned.1.call-update) | async-done | bytes 4194320 | tf_op jit(solution)/shard_map/psum | solution.py:47
  201.6 4.6 convert_reduce_fusion.1
  206.2 0.0 copy-start.4
  206.2 1.0 convert_element_type.73
  207.2 1.0 copy-done.4
  208.2 0.9 fusion.17
  209.0 0.0 all-gather.6.cloned.1.call-update
  209.1 0.0 reduce-scatter.3.cloned.1.call-start
  209.1 54.6 %all-gather.6.cloned.1.call-done = bf16[2048,512]{1,0:T(8,128)(2,1)} async-done(((bf16[256,512]{1,0:T(8,128)(2,1)}), bf16[2048,512]{1,0:T(8,128)(2,1)}) %all-gather.6.cloned.1.call-update) | async-done | bytes 2097168 | tf_op jit(solution)/shard_map/all_gather | solution.py:52
  263.7 0.0 copy-done
  263.7 8.3 %convolution_convert_fusion.1 = bf16[2048,2048]{1,0:T(8,128)(2,1)} fusion(bf16[2048,512]{1,0:T(8,128)(2,1)} %all-gather.6.cloned.1.call-done, bf16[512,2048]{1,0:T(8,128)(2,1)S(1)} %copy-done), kind=kOutput, calls=%fused_computation.12 | convolution fusion | flops 4299161600 | bytes 12582912 | tf_op jit(solution)/shard_map/dot_general | solution.py:54
  272.0 0.0 reduce-scatter.3.cloned.1.call-update
  272.0 0.0 all-gather.8.cloned.1.call-start
  272.1 73.0 %reduce-scatter.3.cloned.1.call-done = bf16[128,2048]{1,0:T(8,128)(2,1)} async-done(((bf16[2048,2048]{1,0:T(8,128)(2,1)}), bf16[128,2048]{1,0:T(8,128)(2,1)}) %reduce-scatter.3.cloned.1.call-update) | async-done | bytes 524304 | tf_op jit(solution)/shard_map/reduce_scatter | solution.py:53
  345.1 2.2 fusion.14
  347.4 0.0 all-gather.8.cloned.1.call-update
  347.4 0.0 reduce-scatter.5.cloned.1.call-start
  347.5 50.4 %all-gather.8.cloned.1.call-done = bf16[2048,2048]{1,0:T(8,128)(2,1)} async-done(((bf16[128,2048]{1,0:T(8,128)(2,1)}), bf16[2048,2048]{1,0:T(8,128)(2,1)}) %all-gather.8.cloned.1.call-update) | async-done | bytes 8388624 | tf_op jit(solution)/shard_map/all_gather | solution.py:61
  397.9 0.0 copy-start.1
  397.9 10.0 %convolution_convert_fusion.2 = bf16[2048,512]{1,0:T(8,128)(2,1)} fusion(bf16[2048,2048]{1,0:T(8,128)(2,1)} %all-gather.8.cloned.1.call-done, bf16[2048,512]{1,0:T(8,128)(2,1)} %param.19), kind=kOutput, calls=%fused_computation.14 | convolution fusion | flops 4296015872 | bytes 12582912 | tf_op jit(solution)/shard_map/dot_general | solution.py:60
  407.9 0.0 reduce-scatter.5.cloned.1.call-update
  407.9 76.0 %reduce-scatter.5.cloned.1.call-done = bf16[256,512]{1,0:T(8,128)(2,1)} async-done(((bf16[2048,512]{1,0:T(8,128)(2,1)}), bf16[256,512]{1,0:T(8,128)(2,1)}) %reduce-scatter.5.cloned.1.call-update) | async-done | bytes 262160 | tf_op jit(solution)/shard_map/reduce_scatter | solution.py:65
  484.0 1.8 add_convert_fusion
  485.8 0.0 copy-done.1
  (2 shorter events, 0.0 us)
Async XLA Ops:
  6.5 257.2 %copy-start = (bf16[512,2048]{1,0:T(8,128)(2,1)S(1)}, bf16[512,2048]{1,0:T(8,128)(2,1)}, u32[]{:S(2)}) copy-start(bf16[512,2048]{1,0:T(8,128)(2,1)} %param.18) | copy-start | bytes 6291460
  6.5 46.0 %copy-start.7 = (f32[8192]{0:T(1024)S(1)}, f32[8192]{0:T(1024)}, u32[]{:S(2)}) copy-start(f32[8192]{0:T(1024)} %param.12) | copy-start | bytes 98308
  6.5 42.4 %all-gather.4.cloned.1.call-start = ((), (), s32[]{:S(2)}) async-start(), calls=%async_computation.2 | async-start | bytes 4456448 | tf_op jit(solution)/shard_map/all_gather | solution.py:23
  7.3 194.3 %all-reduce.2.cloned.1.call-start = ((), (), s32[]{:S(2)}) async-start(), calls=%async_computation.3 | async-start | bytes 8388608 | tf_op jit(solution)/shard_map/psum | solution.py:47
  49.0 3.6 copy-start.3
  52.5 2.2 copy-start.5
  54.7 2.1 copy-start.2
  54.7 3.7 copy-start.6
  71.9 191.8 %all-gather.6.cloned.1.call-start = ((), (), s32[]{:S(2)}) async-start(), calls=%async_computation.4 | async-start | bytes 2359296 | tf_op jit(solution)/shard_map/all_gather | solution.py:52
  206.2 2.0 copy-start.4
  209.1 136.1 %reduce-scatter.3.cloned.1.call-start = ((), (), s32[]{:S(2)}) async-start(), calls=%async_computation.5 | async-start | bytes 8912896 | tf_op jit(solution)/shard_map/reduce_scatter | solution.py:53
  272.0 125.8 %all-gather.8.cloned.1.call-start = ((), (), s32[]{:S(2)}) async-start(), calls=%async_computation.6 | async-start | bytes 8912896 | tf_op jit(solution)/shard_map/all_gather | solution.py:61
  347.4 136.6 %reduce-scatter.5.cloned.1.call-start = ((), (), s32[]{:S(2)}) async-start(), calls=%async_computation.7 | async-start | bytes 2359296 | tf_op jit(solution)/shard_map/reduce_scatter | solution.py:65
  397.9 87.9 %copy-start.1 = (bf16[512,2048]{1,0:T(8,128)(2,1)S(1)}, bf16[512,2048]{1,0:T(8,128)(2,1)}, u32[]{:S(2)}) copy-start(bf16[512,2048]{1,0:T(8,128)(2,1)} %param.18) | copy-start | bytes 6291460
Sparse Core Ops, SparseCore 0:
  9.0 39.8 all-gather.3
  72.0 129.5 all-reduce.1
  209.2 54.4 all-gather.5
  272.2 72.9 reduce-scatter.2
  347.5 50.3 all-gather.7
  408.0 75.8 reduce-scatter.4
where the time goes:
time: 493 us
  waiting for transfers between devices  424 us (86%)
  matrix products  33.5 us (7%)
  other arithmetic  16.6 us (3%)
  between operations  13.6 us (3%)
    psum x1, waiting for transfers between devices, per_device(): lax.psum(partial_out.astype(jnp.bfloat16), ('section', 'tensor'))  129 us
    reduce_scatter x1, waiting for transfers between devices, per_device(): lax.psum_scatter(partial_down.astype(jnp.bfloat16), 'dp', scatter_dimensi...  76 us
    reduce_scatter x1, waiting for transfers between devices, per_device(): lax.psum_scatter(jnp.dot(gathered, w_up, preferred_element_type=jnp.float...  73 us
    all_gather x1, waiting for transfers between devices, per_device(): gathered = lax.all_gather(normed_ffn, 'dp', axis=0, tiled=True)  54.6 us
    all_gather x1, waiting for transfers between devices, per_device(): lax.all_gather(activated, ('section', 'tensor'), axis=0, tiled=True)  50.4 us
    all_gather x1, waiting for transfers between devices, per_device(): whole = lax.all_gather(tokens, ('section', 'tensor'), axis=1, tiled=True)  40.8 us
    dot_general x1, matrix products, per_device(): jnp.dot(lax.all_gather(activated, ('section', 'tensor'), axis=0, tiled=Tr...  9.99 us
  transfers between devices with their start and end apart: 6, of which 6 were waited for; matrix products, arithmetic and copies ran while one was open for 0% of the time, Pallas kernels for 0%

commit v1 on v0

--- a/solution.py
+++ b/solution.py
@@ -4,6 +4,12 @@
 from jax.sharding import PartitionSpec as P
 
 HD = 128
+
+
+def recover_body(raw, which_axis, along_axis):
+    newest = lax.psum(raw, axis_name=which_axis)
+    arr_out = lax.psum(newest, axis_name=along_axis)
+    return arr_out
 
 
 def layer_norm(values, gain):
@@ -44,7 +50,7 @@
     context = jnp.einsum("hqk,khd->qhd", probs, value, preferred_element_type=jnp.float32)
     context = context.astype(jnp.bfloat16).reshape(tok_rows, local_heads * HD)
     partial_out = jnp.dot(context, w_output, preferred_element_type=jnp.float32)
-    summed = lax.psum(partial_out.astype(jnp.bfloat16), ("section", "tensor")).astype(jnp.float32)
+    summed = recover_body(partial_out.astype(jnp.bfloat16), "tensor", "section").astype(jnp.float32)
     resid_full = (whole.astype(jnp.float32) + summed).astype(jnp.bfloat16)
     normed_full = layer_norm(resid_full.astype(jnp.float32), gain_ffn).astype(jnp.bfloat16)
     normed_ffn = lax.dynamic_slice_in_dim(normed_full, first_col, share, 1)

time: 493 us -> 554 us (1.12)
  waiting for transfers between devices: 424 us -> 485 us
    psum x1 -> x2, waiting for transfers between devices: 129 us -> 189 us  [the longest x1 116 us: recover_body(): arr_out = lax.psum(newest, axis_name=along_axis)]
  transfers between devices with their start and end apart: 6 -> 7, of which waited for: 6 -> 7; matrix products, arithmetic and copies ran while one was open for 0% -> 0% of each run, Pallas kernels for 0% -> 0%
where the time goes in v1:
time: 554 us; the launch traced here: 553 us
  waiting for transfers between devices  485 us (88%)
  matrix products  33.5 us (6%)
  other arithmetic  16.6 us (3%)
  between operations  13.6 us (2%)
    psum x1, waiting for transfers between devices, recover_body(): arr_out = lax.psum(newest, axis_name=along_axis)  116 us
    reduce_scatter x1, waiting for transfers between devices, per_device(): lax.psum_scatter(partial_down.astype(jnp.bfloat16), 'dp', scatter_dimensi...  76.1 us
    reduce_scatter x1, waiting for transfers between devices, per_device(): lax.psum_scatter(jnp.dot(gathered, w_up, preferred_element_type=jnp.float...  73.1 us
    psum x1, waiting for transfers between devices, recover_body(): newest = lax.psum(raw, axis_name=which_axis)  73 us
    all_gather x1, waiting for transfers between devices, per_device(): gathered = lax.all_gather(normed_ffn, 'dp', axis=0, tiled=True)  54.9 us
    all_gather x1, waiting for transfers between devices, per_device(): lax.all_gather(activated, ('section', 'tensor'), axis=0, tiled=True)  50.4 us
    all_gather x1, waiting for transfers between devices, per_device(): whole = lax.all_gather(tokens, ('section', 'tensor'), axis=1, tiled=True)  40.8 us
  transfers between devices with their start and end apart: 7, of which 7 were waited for; matrix products, arithmetic and copies ran while one was open for 0% of the time, Pallas kernels for 0%

profile of v1, /device:TPU:0, one launch (start us, length us, event | category | flops | bytes accessed | tf_op | source)
XLA Modules:
  0.0 553.3 jit_solution(15051552502903201443)
XLA Ops:
  6.5 0.0 copy-start
  6.5 0.0 copy-start.7
  6.5 0.0 all-gather.4.cloned.1.call-start
  6.5 0.7 all-gather.4.cloned.1.call-update
  7.3 0.0 all-reduce.3.cloned.1.call-start
  7.3 0.9 fusion.18
  8.2 40.8 %all-gather.4.cloned.1.call-done = bf16[256,8192]{1,0:T(8,128)(2,1)} async-done(((bf16[256,512]{1,0:T(8,128)(2,1)}), bf16[256,8192]{1,0:T(8,128)(2,1)}) %all-gather.4.cloned.1.call-update) | async-done | bytes 4194320 | tf_op jit(solution)/shard_map/all_gather | solution.py:29
  49.0 0.0 copy-start.3
  49.0 3.5 convert_reduce_fusion
  52.5 0.0 copy-done.7
  52.5 0.0 copy-done.3
  52.5 0.0 copy-start.5
  52.5 1.8 fusion.3
  54.3 0.4 copy-done.5
  54.7 0.0 copy-start.2
  54.7 0.0 copy-start.6
  54.7 1.8 convolution_convert_fusion.4
  56.6 0.3 copy-done.2
  56.9 1.6 copy-done.6
  58.4 1.8 convolution_convert_fusion.5
  60.3 0.4 fusion.23
  60.7 0.3 fusion.8
  60.9 5.2 convolution_convert_fusion.6
  66.1 0.3 convolution_convert_fusion.3
  66.4 5.4 convolution_convert_fusion
  71.9 0.0 all-reduce.3.cloned.1.call-update
  71.9 0.0 all-reduce.5.cloned.1.call-start
  71.9 73.0 %all-reduce.3.cloned.1.call-done = bf16[256,8192]{1,0:T(8,128)(2,1)} async-done(((bf16[256,8192]{1,0:T(8,128)(2,1)}), bf16[256,8192]{1,0:T(8,128)(2,1)}) %all-reduce.3.cloned.1.call-update) | async-done | bytes 4194320 | tf_op jit(solution)/shard_map/psum | solution.py:10
  145.0 0.0 all-reduce.5.cloned.1.call-update
  145.0 0.2 all-gather.6.cloned.1.call-start
  145.2 0.8 dynamic-slice
  146.0 115.9 %all-reduce.5.cloned.1.call-done = bf16[256,8192]{1,0:T(8,128)(2,1)} async-done(((bf16[256,8192]{1,0:T(8,128)(2,1)}), bf16[256,8192]{1,0:T(8,128)(2,1)}) %all-reduce.5.cloned.1.call-update) | async-done | bytes 4194320 | tf_op jit(solution)/shard_map/psum | solution.py:11
  261.9 4.6 convert_reduce_fusion.1
  266.5 0.0 copy-start.4
  266.5 1.0 convert_element_type.73
  267.5 1.0 copy-done.4
  268.5 0.9 fusion.17
  269.4 0.0 all-gather.6.cloned.1.call-update
  269.4 0.0 reduce-scatter.3.cloned.1.call-start
  269.4 54.9 %all-gather.6.cloned.1.call-done = bf16[2048,512]{1,0:T(8,128)(2,1)} async-done(((bf16[256,512]{1,0:T(8,128)(2,1)}), bf16[2048,512]{1,0:T(8,128)(2,1)}) %all-gather.6.cloned.1.call-update) | async-done | bytes 2097168 | tf_op jit(solution)/shard_map/all_gather | solution.py:58
  324.4 0.0 copy-done
  324.4 8.3 %convolution_convert_fusion.1 = bf16[2048,2048]{1,0:T(8,128)(2,1)} fusion(bf16[2048,512]{1,0:T(8,128)(2,1)} %all-gather.6.cloned.1.call-done, bf16[512,2048]{1,0:T(8,128)(2,1)S(1)} %copy-done), kind=kOutput, calls=%fused_computation.12 | convolution fusion | flops 4299161600 | bytes 12582912 | tf_op jit(solution)/shard_map/dot_general | solution.py:60
  332.7 0.0 reduce-scatter.3.cloned.1.call-update
  332.7 0.0 all-gather.8.cloned.1.call-start
  332.8 73.1 %reduce-scatter.3.cloned.1.call-done = bf16[128,2048]{1,0:T(8,128)(2,1)} async-done(((bf16[2048,2048]{1,0:T(8,128)(2,1)}), bf16[128,2048]{1,0:T(8,128)(2,1)}) %reduce-scatter.3.cloned.1.call-update) | async-done | bytes 524304 | tf_op jit(solution)/shard_map/reduce_scatter | solution.py:59
  405.9 2.2 fusion.14
  408.1 0.0 all-gather.8.cloned.1.call-update
  408.1 0.0 reduce-scatter.5.cloned.1.call-start
  408.2 50.4 %all-gather.8.cloned.1.call-done = bf16[2048,2048]{1,0:T(8,128)(2,1)} async-done(((bf16[128,2048]{1,0:T(8,128)(2,1)}), bf16[2048,2048]{1,0:T(8,128)(2,1)}) %all-gather.8.cloned.1.call-update) | async-done | bytes 8388624 | tf_op jit(solution)/shard_map/all_gather | solution.py:67
  458.6 0.0 copy-start.1
  458.6 10.0 %convolution_convert_fusion.2 = bf16[2048,512]{1,0:T(8,128)(2,1)} fusion(bf16[2048,2048]{1,0:T(8,128)(2,1)} %all-gather.8.cloned.1.call-done, bf16[2048,512]{1,0:T(8,128)(2,1)} %param.19), kind=kOutput, calls=%fused_computation.14 | convolution fusion | flops 4296015872 | bytes 12582912 | tf_op jit(solution)/shard_map/dot_general | solution.py:66
  468.6 0.0 reduce-scatter.5.cloned.1.call-update
  468.6 76.1 %reduce-scatter.5.cloned.1.call-done = bf16[256,512]{1,0:T(8,128)(2,1)} async-done(((bf16[2048,512]{1,0:T(8,128)(2,1)}), bf16[256,512]{1,0:T(8,128)(2,1)}) %reduce-scatter.5.cloned.1.call-update) | async-done | bytes 262160 | tf_op jit(solution)/shard_map/reduce_scatter | solution.py:71
  544.7 1.8 add_convert_fusion
  546.4 0.0 copy-done.1
  (2 shorter events, 0.0 us)
Async XLA Ops:
  6.5 317.9 %copy-start = (bf16[512,2048]{1,0:T(8,128)(2,1)S(1)}, bf16[512,2048]{1,0:T(8,128)(2,1)}, u32[]{:S(2)}) copy-start(bf16[512,2048]{1,0:T(8,128)(2,1)} %param.18) | copy-start | bytes 6291460
  6.5 46.0 %copy-start.7 = (f32[8192]{0:T(1024)S(1)}, f32[8192]{0:T(1024)}, u32[]{:S(2)}) copy-start(f32[8192]{0:T(1024)} %param.12) | copy-start | bytes 98308
  6.5 42.4 %all-gather.4.cloned.1.call-start = ((), (), s32[]{:S(2)}) async-start(), calls=%async_computation.2 | async-start | bytes 4456448 | tf_op jit(solution)/shard_map/all_gather | solution.py:29
  7.3 137.7 %all-reduce.3.cloned.1.call-start = ((), (), s32[]{:S(2)}) async-start(), calls=%async_computation.3 | async-start | bytes 8388608 | tf_op jit(solution)/shard_map/psum | solution.py:10
  49.0 3.6 copy-start.3
  52.5 2.2 copy-start.5
  54.7 2.1 copy-start.2
  54.7 3.7 copy-start.6
  71.9 190.0 %all-reduce.5.cloned.1.call-start = ((), (), s32[]{:S(2)}) async-start(), calls=%async_computation.4 | async-start | bytes 8388608 | tf_op jit(solution)/shard_map/psum | solution.py:11
  145.0 179.4 %all-gather.6.cloned.1.call-start = ((), (), s32[]{:S(2)}) async-start(), calls=%async_computation.5 | async-start | bytes 2359296 | tf_op jit(solution)/shard_map/all_gather | solution.py:58
  266.5 2.0 copy-start.4
  269.4 136.5 %reduce-scatter.3.cloned.1.call-start = ((), (), s32[]{:S(2)}) async-start(), calls=%async_computation.6 | async-start | bytes 8912896 | tf_op jit(solution)/shard_map/reduce_scatter | solution.py:59
  332.7 125.8 %all-gather.8.cloned.1.call-start = ((), (), s32[]{:S(2)}) async-start(), calls=%async_computation.7 | async-start | bytes 8912896 | tf_op jit(solution)/shard_map/all_gather | solution.py:67
  408.1 136.5 %reduce-scatter.5.cloned.1.call-start = ((), (), s32[]{:S(2)}) async-start(), calls=%async_computation.8 | async-start | bytes 2359296 | tf_op jit(solution)/shard_map/reduce_scatter | solution.py:71
  458.6 87.9 %copy-start.1 = (bf16[512,2048]{1,0:T(8,128)(2,1)S(1)}, bf16[512,2048]{1,0:T(8,128)(2,1)}, u32[]{:S(2)}) copy-start(bf16[512,2048]{1,0:T(8,128)(2,1)} %param.18) | copy-start | bytes 6291460
Sparse Core Ops, SparseCore 0:
  9.0 39.8 all-gather.3
  72.0 72.9 all-reduce.2
  147.6 114.3 all-reduce.4
  269.5 54.8 all-gather.5
  332.8 72.9 reduce-scatter.2
  408.2 50.2 all-gather.7
  468.7 75.8 reduce-scatter.4
